TPU v7x, 512 devices: a whole 4x4x16 slice. The times are simulated.
512 devices in a mesh: tri: 64 (over y, z), sub: 8 (over x, core).
Axes of the slice: x: 4, y: 4, z: 16, core: 2. Of those that a mesh axis runs over, the one named last changes fastest.
Arguments:
- stored_tiles: float32 [64, 10, 512, 512], P('tri', None, 'sub'), may hold values from -190 to 190, as said below
- cell_owner: int32 [64], replicated, may hold values from 0 to 63, as said below
Outputs:
- updated: float32 [64, 10, 512, 512], P('tri', None, 'sub')
Inputs may be any that keep to these rules, and one draw needn't show every extreme that they name: `cell_owner`: a permutation of the indices of tri. `stored_tiles`: every tile whose row and column blocks are equal is skew-symmetric, every pivot met is invertible, and slots that hold no tile are zero.
All inputs are finite; a program needn't handle non-finite values.
Results may differ from a plain program's by a relative error of at most 0.00035.
Values may be sent and summed in bfloat16 or wider, within the bound.
A program may use at most 64 MiB of HBM per device.

v0:
```python
import math
import jax
import jax.numpy as jnp
import numpy as np
from jax import lax
from jax.sharding import Mesh
from jax.sharding import PartitionSpec as P

NB = 32
TRI = ("tri_0", "tri_1")


def in_order(tiles, dim):
    tiles = jnp.moveaxis(tiles, 0, dim)
    dims = tiles.shape
    return tiles.reshape(*dims[:dim], dims[dim] * dims[dim + 1], *dims[dim + 2 :])


def gather_in_order(x, axes, turns):
    tiles = x[None]
    for k in turns:
        tiles = lax.all_gather(tiles, axes[k], axis=0, tiled=True)
    block = [lax.axis_size(axes[k]) for k in reversed(turns)]
    tiles = tiles.reshape(*block, *x.shape)
    turned = sorted(range(len(turns)), key=lambda place: turns[len(turns) - 1 - place])
    return tiles.transpose(*turned, *range(len(turns), tiles.ndim)).reshape(-1, *x.shape)


def gather_axes(x, axes, turns, dim):
    return in_order(gather_in_order(x, axes, turns), dim)


def layout(groups, per_group):
    half_group = per_group // 2
    slot_count = per_group * (per_group + 1) // 2
    row_table = np.full((groups * groups, slot_count), -1, np.int32)
    col_table = np.full((groups * groups, slot_count), -1, np.int32)
    for first_group in range(groups):
        for second_group in range(groups):
            cell_index = first_group * groups + second_group
            for inner_row in range(per_group):
                if first_group == second_group:
                    for inner_column in range(inner_row + 1):
                        slot_index = inner_row * (inner_row + 1) // 2 + inner_column
                        row_table[cell_index, slot_index] = first_group * per_group + inner_row
                        col_table[cell_index, slot_index] = first_group * per_group + inner_column
                else:
                    for inner_column in range(half_group):
                        slot_index = inner_row * half_group + inner_column
                        if first_group > second_group:
                            row_table[cell_index, slot_index] = first_group * per_group + inner_row
                            col_table[cell_index, slot_index] = (
                                second_group * per_group + inner_column
                            )
                        else:
                            row_table[cell_index, slot_index] = second_group * per_group + inner_row
                            col_table[cell_index, slot_index] = (
                                first_group * per_group + half_group + inner_column
                            )
    return (row_table, col_table)


def shards(stored_tiles, cell_owner):
    tri_count = lax.axis_size(TRI)
    groups = math.isqrt(tri_count)
    per_group = NB // groups
    half_group = per_group // 2
    strip_rows = stored_tiles.shape[2]
    block_order = stored_tiles.shape[3]
    row_table, col_table = layout(groups, per_group)
    position = lax.axis_index(TRI)
    my_cell = jnp.sum(jnp.where(cell_owner == position, jnp.arange(tri_count, dtype=jnp.int32), 0))
    cell_down = my_cell // groups
    cell_across = my_cell % groups
    row_group = jnp.maximum(cell_down, cell_across)
    col_group = jnp.minimum(cell_down, cell_across)
    my_rows = jnp.asarray(row_table)[my_cell]
    my_cols = jnp.asarray(col_table)[my_cell]
    row_local = jnp.clip(my_rows - row_group * per_group, 0, per_group - 1)
    col_local = jnp.clip(my_cols - col_group * per_group, 0, per_group - 1)
    holders = cell_owner[jnp.arange(groups) * groups]
    highest = lax.Precision.HIGHEST
    current = stored_tiles[0]
    lower_slots = np.array([member * half_group for member in range(per_group)], np.int32)
    first_slots = np.array(
        [member * (member + 1) // 2 if member > 0 else 0 for member in range(per_group)], np.int32
    )
    keep_first = np.array([1.0 if member > 0 else 0.0 for member in range(per_group)], np.float32)
    from_lower = current[lower_slots]
    from_first = current[first_slots] * keep_first[:, None, None]
    holder_part = jnp.where(cell_down > 0, from_lower, from_first)
    holder_part = jnp.where(cell_across == 0, holder_part, 0.0).astype(jnp.bfloat16)
    pivot_slot = 0 // 2
    pivot_part = jnp.where(my_cell == 0, current[pivot_slot], 0.0)
    piece_size = holder_part.size // tri_count
    spread_panel = lax.all_to_all(
        holder_part.reshape(tri_count, piece_size), TRI, split_axis=0, concat_axis=0, tiled=True
    )
    spread_pivot = lax.all_to_all(
        pivot_part.astype(jnp.bfloat16), TRI, split_axis=0, concat_axis=0, tiled=True
    ).astype(pivot_part.dtype)
    picked_panel = spread_panel[holders][:, None, :]
    picked_pivot = spread_pivot[holders[0]][None, :]
    whole_panel = gather_axes(picked_panel, TRI, (0, 1), 1)
    whole_pivot = gather_axes(picked_pivot.astype(jnp.bfloat16), TRI, (0, 1), 0).astype(
        picked_pivot.dtype
    )
    panels = whole_panel.reshape(groups, per_group, strip_rows, block_order)
    own_strips = panels[row_group]
    other_strips = panels[col_group]
    pivot_block = lax.all_gather(
        whole_pivot.astype(jnp.bfloat16), "sub", axis=0, tiled=True
    ).astype(whole_pivot.dtype)
    partner = lax.all_gather(other_strips, "sub", axis=1, tiled=True)
    gram_matrix = jnp.dot(pivot_block.T, pivot_block, precision=highest)
    factor = jnp.linalg.cholesky(gram_matrix)
    inverse = jax.scipy.linalg.cho_solve((factor, True), pivot_block.T)
    scaled = jnp.einsum(
        "irk,kc->irc", own_strips.astype(jnp.float32), inverse, precision=highest
    ).astype(jnp.bfloat16)
    left_slots = scaled[row_local]
    right_slots = partner[col_local]
    update = jnp.einsum("qrk,qck->qrc", left_slots, right_slots, preferred_element_type=jnp.float32)
    live_slots = (my_rows > 0) & (my_cols > 0)
    current = current + jnp.where(live_slots[:, None, None], update, 0.0)
    return current[None]


def solution(mesh):
    torus = Mesh(mesh.devices.reshape(4, 16, mesh.shape["sub"]), ("tri_0", "tri_1", "sub"))
    return jax.shard_map(
        shards,
        mesh=torus,
        in_specs=(P(TRI, None, "sub", None), P()),
        out_specs=P(TRI, None, "sub", None),
        check_vma=False,
    )
```

profile of v0, /device:TPU:1, one launch (start us, length us, event | category | flops | bytes accessed | tf_op | source)
XLA Modules:
  0.0 323.7 jit_solution(5538113034983923474)
XLA Ops:
  6.5 1.4 fusion.56
  8.6 0.9 fusion.39
  10.6 0.6 reshape.305
  11.3 19.3 %all-to-all-start.1 = ((bf16[64,2,256]{2,1,0:T(2,128)(2,1)}), bf16[64,2,256]{2,1,0:T(2,128)(2,1)S(1)}, u32[]{:S(2)}, u32[]{:S(2)}) async-start(bf16[64,2,256]{2,1,0:T(2,128)(2,1)} %reshape.305), calls=%async_computation.1 | async-start | bytes 131072 | tf_op jit(solution)/shard_map/all_to_all | solution.py:99
  33.4 1.3 gather_fusion.2
  34.7 0.7 pad_clamp_fusion.4
  35.4 1.9 gather_fusion.1
  37.3 1.9 gather_fusion
  40.6 0.7 fusion.59
  41.3 0.7 and_bitcast_fusion
  42.2 0.7 fusion.60
  43.2 2.1 reduce.26
  45.2 0.9 reshape.307
  46.2 14.6 %all-to-all-start = ((bf16[64,2,1024]{2,1,0:T(2,128)(2,1)}), bf16[64,2,1024]{2,1,0:T(2,128)(2,1)S(1)}, u32[]{:S(2)}, u32[]{:S(2)}) async-start(bf16[64,2,1024]{2,1,0:T(2,128)(2,1)} %reshape.307), calls=%async_computation | async-start | bytes 524288 | tf_op jit(solution)/shard_map/all_to_all | solution.py:96
  60.9 8.8 %all_gather.20 = bf16[4,1,512]{2,1,0:T(2,128)(2,1)S(1)} all-gather(bf16[1,1,512]{2,1,0:T(2,128)(2,1)S(1)} %fusion.54), channel_id=1, replica_groups=mesh['tri_0'=4,'tri_1'=16,'sub'=8] {'tri_0'}, dimensions={0}, use_global_device_ids=true | all-gather | bytes 5120 | tf_op jit(solution)/shard_map/all_gather | solution.py:22
  69.7 23.8 %all_gather.21 = bf16[64,1,512]{2,1,0:T(2,128)(2,1)S(1)} all-gather(bf16[4,1,512]{2,1,0:T(2,128)(2,1)S(1)} %all_gather.20), channel_id=1, replica_groups=mesh['tri_0'=4,'tri_1'=16,'sub'=8] {'tri_1'}, dimensions={0}, use_global_device_ids=true | all-gather | bytes 69632 | tf_op jit(solution)/shard_map/all_gather | solution.py:22
  93.9 23.9 %all_gather.22 = bf16[512,512]{1,0:T(8,128)(2,1)S(1)} all-gather(bf16[64,512]{1,0:T(8,128)(2,1)S(1)} %bitcast.120), channel_id=1, replica_groups=mesh['tri_0'=4,'tri_1'=16,'sub'=8] {'sub'}, dimensions={0}, use_global_device_ids=true | all-gather | bytes 589824 | tf_op jit(solution)/shard_map/all_gather | solution.py:111
  118.9 1.0 copy-done.1
  119.9 11.7 %cholesky.104 = f32[128,128]{1,0:T(8,128)S(1)} custom-call(f32[128,128]{1,0:T(8,128)S(1)} %cholesky.266), custom_call_target="Cholesky" | custom-call | tf_op jit(solution)/shard_map/jit(cholesky)/cholesky | solution.py:116
  131.6 9.8 %custom-call.34 = f32[1,128,128]{1,2,0:T(8,128)S(1)} custom-call(f32[1,128,128]{2,1,0:T(8,128)S(1)} %get-tuple-element.32), custom_call_target="InvertDiagBlocksLowerTriangular" | custom-call | tf_op jit(solution)/shard_map/jit(cholesky)/cholesky | solution.py:116
  142.6 9.8 %all-gather = bf16[32,2048]{1,0:T(8,128)(2,1)} all-gather(bf16[8,2048]{1,0:T(8,128)(2,1)S(1)} %gather_fusion.3), channel_id=2, replica_groups=mesh['tri_0'=4,'tri_1'=16,'sub'=8] {'tri_0'}, dimensions={0}, use_global_device_ids=true | all-gather | bytes 163840 | tf_op jit(solution)/shard_map/all_gather | solution.py:22
  153.0 1.0 copy.32
  154.3 11.7 %cholesky.217 = f32[128,128]{1,0:T(8,128)S(1)} custom-call(f32[128,128]{1,0:T(8,128)S(1)} %cholesky.270), custom_call_target="Cholesky" | custom-call | tf_op jit(solution)/shard_map/jit(cholesky)/cholesky | solution.py:116
  166.1 9.8 %custom-call.35 = f32[1,128,128]{1,2,0:T(8,128)S(1)} custom-call(f32[1,128,128]{2,1,0:T(8,128)S(1)} %get-tuple-element.29), custom_call_target="InvertDiagBlocksLowerTriangular" | custom-call | tf_op jit(solution)/shard_map/jit(cholesky)/cholesky | solution.py:116
  176.6 11.7 %cholesky.238 = f32[128,128]{1,0:T(8,128)S(1)} custom-call(f32[128,128]{1,0:T(8,128)S(1)} %cholesky.275), custom_call_target="Cholesky" | custom-call | tf_op jit(solution)/shard_map/jit(cholesky)/cholesky | solution.py:116
  188.3 10.0 %custom-call.36 = f32[1,128,128]{1,2,0:T(8,128)S(1)} custom-call(f32[1,128,128]{2,1,0:T(8,128)S(1)} %get-tuple-element.26), custom_call_target="InvertDiagBlocksLowerTriangular" | custom-call | tf_op jit(solution)/shard_map/jit(cholesky)/cholesky | solution.py:116
  198.9 11.7 %cholesky.255 = f32[128,128]{1,0:T(8,128)S(1)} custom-call(f32[128,128]{1,0:T(8,128)S(1)} %convolution_subtract_fusion.8), custom_call_target="Cholesky" | custom-call | tf_op jit(solution)/shard_map/jit(cholesky)/cholesky | solution.py:116
  210.6 0.7 compare_reduce_fusion.2
  212.7 0.7 compare_reduce_fusion.1
  214.1 0.7 compare_reduce_fusion
  215.7 10.8 %while.1 = (s32[]{:T(128)}, f32[512,512]{1,0:T(8,128)S(1)}, s32[4,2]{0,1:T(2,128)S(1)}, f32[4,128,128]{2,1,0:T(8,128)}, s32[]{:T(128)}) while((s32[]{:T(128)}, f32[512,512]{1,0:T(8,128)S(1)}, s32[4,2]{0,1:T(2,128)S(1)}, f32[4,128,128]{2,1,0:T(8,128)}, s32[]{:T(128)}) %tuple.27), condition=%wide.while_cond, body=%wide.while_body.sunk | while | flops 2 | bytes 132705 | solution.py:117
  216.4 2.0 bitcast_dynamic-update-slice_fusion.2
  219.1 2.0 bitcast_dynamic-update-slice_fusion.2
  221.8 2.0 bitcast_dynamic-update-slice_fusion.2
  224.5 2.0 bitcast_dynamic-update-slice_fusion.2
  226.5 40.1 %custom-call.37 = f32[4,128,128]{1,2,0:T(8,128)S(1)} custom-call(f32[4,128,128]{2,1,0:T(8,128)} %get-tuple-element.12), custom_call_target="InvertDiagBlocksLowerTriangular" | custom-call | tf_op jit(solution)/shard_map/jit(_cho_solve)/triangular_solve | solution.py:117
  266.7 1.7 copy.27
  268.4 1.2 copy.28
  269.6 2.6 reshape_reshape.6
  272.2 1.7 constant_dynamic-slice_fusion.1
  273.9 1.2 fusion.35
  275.1 1.2 bitcast_convert_fusion
  278.0 0.6 convolution_subtract_fusion.5
  281.0 0.7 convolution_subtract_fusion.4
  282.1 1.6 convolution_convert_fusion
  284.3 21.5 %all-gather.7.cloned.1.call-done = bf16[1,4,512,512]{3,2,1,0:T(8,128)(2,1)} async-done(((bf16[1,4,64,512]{3,2,1,0:T(8,128)(2,1)}), bf16[1,4,512,512]{3,2,1,0:T(8,128)(2,1)}) %all-gather.7.cloned.1.call-update) | async-done | bytes 2097168 | tf_op jit(solution)/shard_map/all_gather | solution.py:114
  305.8 5.5 %gather_fusion.5 = bf16[10,512,512]{2,1,0:T(8,128)(2,1)} fusion(bf16[4,512,512]{2,1,0:T(8,128)(2,1)} %bitcast.112, s32[1024]{0:T(1024)S(1)} %pad_clamp_fusion), kind=kCustom, calls=%fused_computation.5 | custom fusion | bytes 10485800 | tf_op jit(solution)/shard_map/gather | solution.py:122
  311.4 5.2 %fusion.1 = f32[1,10,64,512]{3,2,1,0:T(8,128)} fusion(bf16[10,64,512]{2,1,0:T(8,128)(2,1)S(1)} %gather_fusion.4, bf16[10,512,512]{2,1,0:T(8,128)(2,1)} %gather_fusion.5, pred[10]{0:T(512)(128)(4,1)S(1)} %and_bitcast_fusion, f32[1,10,64,512]{3,2,1,0:T(8,128)S(1)} %copy-done), kind=kOutput, calls=%fused_computation.10 | convolution fusion | flops 336199680 | bytes 8519690 | tf_op jit(solution)/shard_map/qrk,qck->qrc/dot_general | solution.py:123
  (75 shorter events, 14.2 us)
Async XLA Ops:
  6.5 35.5 %copy-start.3 = (f32[4]{0:T(128)S(1)}, f32[4]{0:T(128)}, u32[]{:S(2)}) copy-start(f32[4]{0:T(128)} %constant.245) | copy-start | bytes 52
  11.3 34.9 %all-to-all-start.1 = ((bf16[64,2,256]{2,1,0:T(2,128)(2,1)}), bf16[64,2,256]{2,1,0:T(2,128)(2,1)S(1)}, u32[]{:S(2)}, u32[]{:S(2)}) async-start(bf16[64,2,256]{2,1,0:T(2,128)(2,1)} %reshape.305), calls=%async_computation.1 | async-start | bytes 131072 | tf_op jit(solution)/shard_map/all_to_all | solution.py:99
  46.2 95.4 %all-to-all-start = ((bf16[64,2,1024]{2,1,0:T(2,128)(2,1)}), bf16[64,2,1024]{2,1,0:T(2,128)(2,1)S(1)}, u32[]{:S(2)}, u32[]{:S(2)}) async-start(bf16[64,2,1024]{2,1,0:T(2,128)(2,1)} %reshape.307), calls=%async_computation | async-start | bytes 524288 | tf_op jit(solution)/shard_map/all_to_all | solution.py:96
  60.8 205.9 %all-gather.5.cloned.1.call-start = ((), (), s32[]{:S(2)}) async-start(), calls=%async_computation.2 | async-start | bytes 2228224 | tf_op jit(solution)/shard_map/all_gather | solution.py:22
  118.9 1.0 copy-start.1
  119.9 32.8 %copy-start.2 = (f32[512,512]{1,0:T(8,128)S(1)}, f32[512,512]{1,0:T(8,128)}, u32[]{:S(2)}) copy-start(f32[512,512]{1,0:T(8,128)} %copy-done.1) | copy-start | bytes 3145732
  152.4 153.4 %all-gather.7.cloned.1.call-start = ((), (), s32[]{:S(2)}) async-start(), calls=%async_computation.3 | async-start | bytes 2359296 | tf_op jit(solution)/shard_map/all_gather | solution.py:114
  305.8 5.6 %copy-start = (f32[1,10,64,512]{3,2,1,0:T(8,128)S(1)}, f32[1,10,64,512]{3,2,1,0:T(8,128)}, u32[]{:S(2)}) copy-start(f32[1,10,64,512]{3,2,1,0:T(8,128)} %param.9) | copy-start | bytes 3932164
Sparse Core Ops, SparseCore 0:
  152.6 63.2 all-gather.4
  274.0 31.7 all-gather.6
where the time goes:
time: 329 us; the launch traced here: 324 us
  other arithmetic  129 us (39%)
  blocking collectives  66.3 us (20%)
  local copies, waits for them, and re-layouts  34.9 us (11%)
  starting transfers between devices  34.1 us (10%)
  between operations  21.9 us (7%)
  waiting for transfers between devices  21.6 us (7%)
  matrix products  16.1 us (5%)
    another operation x14, other arithmetic, shards(): factor = jnp.linalg.cholesky(gram_matrix)  78.8 us
    all_gather x3, blocking collectives, gather_in_order(): tiles = lax.all_gather(tiles, axes[k], axis=0, tiled=True)  42.5 us
    another operation x3, other arithmetic, shards(): inverse = jax.scipy.linalg.cho_solve((factor, True), pivot_block.T)  40.3 us
    all_gather x1, blocking collectives, shards(): lax.all_gather(whole_pivot.astype(jnp.bfloat16), 'sub', axis=0, tiled=True)  23.9 us
    all_gather x1, waiting for transfers between devices, shards(): partner = lax.all_gather(other_strips, 'sub', axis=1, tiled=True)  21.5 us
    all_to_all x1, starting transfers between devices, shards(): lax.all_to_all(pivot_part.astype(jnp.bfloat16), TRI, split_axis=0, concat...  19.3 us
    all_to_all x1, starting transfers between devices, shards(): lax.all_to_all(holder_part.reshape(tri_count, piece_size), TRI, split_axi...  14.6 us
    another operation x12, local copies, waits for them, and re-layouts  10.8 us
  transfers between devices with their start and end apart: 4, of which 1 were waited for; matrix products, arithmetic and copies ran while one was open for 48% of the time, Pallas kernels for 0%

commit v1 on v0

--- a/solution.py
+++ b/solution.py
@@ -111,7 +111,12 @@
     pivot_block = lax.all_gather(
         whole_pivot.astype(jnp.bfloat16), "sub", axis=0, tiled=True
     ).astype(whole_pivot.dtype)
-    partner = lax.all_gather(other_strips, "sub", axis=1, tiled=True)
+    ring = [other_strips]
+    for hop in range(7):
+        ring.append(lax.ppermute(ring[-1], "sub", [(dev, (dev + 1) % 8) for dev in range(8)]))
+    partner = jnp.roll(
+        jnp.concatenate(ring[::-1], axis=1), (lax.axis_index("sub") + 1) * ring[0].shape[1], axis=1
+    )
     gram_matrix = jnp.dot(pivot_block.T, pivot_block, precision=highest)
     factor = jnp.linalg.cholesky(gram_matrix)
     inverse = jax.scipy.linalg.cho_solve((factor, True), pivot_block.T)

time: 329 us -> 348 us (1.058)
  the two profiles are of different devices: /device:TPU:1 before, /device:TPU:8 now
where the time goes in v1:
time: 348 us; the launch traced here: 343 us
  other arithmetic  130 us (37%)
  blocking collectives  67 us (19%)
  waiting for transfers between devices  35.6 us (10%)
  local copies, waits for them, and re-layouts  33.9 us (10%)
  starting transfers between devices  33.9 us (10%)
  between operations  21.6 us (6%)
  matrix products  20.8 us (6%)
    another operation x15, other arithmetic, shards(): factor = jnp.linalg.cholesky(gram_matrix)  79.1 us
    all_gather x3, blocking collectives, gather_in_order(): tiles = lax.all_gather(tiles, axes[k], axis=0, tiled=True)  53 us
    another operation x3, other arithmetic, shards(): inverse = jax.scipy.linalg.cho_solve((factor, True), pivot_block.T)  40.3 us
    ppermute x7, waiting for transfers between devices, shards(): lax.ppermute(ring[-1], 'sub', [(dev, (dev + 1) % 8) for dev in range(8)])  35.6 us
    all_to_all x1, starting transfers between devices, shards(): lax.all_to_all(pivot_part.astype(jnp.bfloat16), TRI, split_axis=0, concat...  18.7 us
    all_to_all x1, starting transfers between devices, shards(): lax.all_to_all(holder_part.reshape(tri_count, piece_size), TRI, split_axi...  15.1 us
    all_gather x1, blocking collectives, shards(): lax.all_gather(whole_pivot.astype(jnp.bfloat16), 'sub', axis=0, tiled=True)  13.9 us
    another operation x14, matrix products, shards(): inverse = jax.scipy.linalg.cho_solve((factor, True), pivot_block.T)  10.5 us
  transfers between devices with their start and end apart: 10, of which 7 were waited for; matrix products, arithmetic and copies ran while one was open for 47% of the time, Pallas kernels for 0%

profile of v1, /device:TPU:8, one launch (start us, length us, event | category | flops | bytes accessed | tf_op | source)
XLA Modules:
  0.0 342.7 jit_solution(9222917224167894235)
XLA Ops:
  6.5 1.4 fusion.56
  11.3 18.7 %all-to-all-start.1 = ((bf16[64,2,256]{2,1,0:T(2,128)(2,1)}), bf16[64,2,256]{2,1,0:T(2,128)(2,1)S(1)}, u32[]{:S(2)}, u32[]{:S(2)}) async-start(bf16[64,2,256]{2,1,0:T(2,128)(2,1)} %reshape.304), calls=%async_computation.1 | async-start | bytes 131072 | tf_op jit(solution)/shard_map/all_to_all | solution.py:99
  33.5 1.9 gather_fusion.1
  35.4 1.9 gather_fusion
  37.3 1.3 gather_fusion.2
  43.2 2.1 reduce.26
  46.3 15.1 %all-to-all-start = ((bf16[64,2,1024]{2,1,0:T(2,128)(2,1)}), bf16[64,2,1024]{2,1,0:T(2,128)(2,1)S(1)}, u32[]{:S(2)}, u32[]{:S(2)}) async-start(bf16[64,2,1024]{2,1,0:T(2,128)(2,1)} %reshape.306), calls=%async_computation | async-start | bytes 524288 | tf_op jit(solution)/shard_map/all_to_all | solution.py:96
  61.5 10.9 %all_gather.17 = bf16[4,1,512]{2,1,0:T(2,128)(2,1)S(1)} all-gather(bf16[1,1,512]{2,1,0:T(2,128)(2,1)S(1)} %fusion.54), channel_id=1, replica_groups=mesh['tri_0'=4,'tri_1'=16,'sub'=8] {'tri_0'}, dimensions={0}, use_global_device_ids=true | all-gather | bytes 5120 | tf_op jit(solution)/shard_map/all_gather | solution.py:22
  72.5 29.9 %all_gather.18 = bf16[64,1,512]{2,1,0:T(2,128)(2,1)S(1)} all-gather(bf16[4,1,512]{2,1,0:T(2,128)(2,1)S(1)} %all_gather.17), channel_id=1, replica_groups=mesh['tri_0'=4,'tri_1'=16,'sub'=8] {'tri_1'}, dimensions={0}, use_global_device_ids=true | all-gather | bytes 69632 | tf_op jit(solution)/shard_map/all_gather | solution.py:22
  102.8 13.9 %all_gather.19 = bf16[512,512]{1,0:T(8,128)(2,1)S(1)} all-gather(bf16[64,512]{1,0:T(8,128)(2,1)S(1)} %bitcast.124), channel_id=1, replica_groups=mesh['tri_0'=4,'tri_1'=16,'sub'=8] {'sub'}, dimensions={0}, use_global_device_ids=true | all-gather | bytes 589824 | tf_op jit(solution)/shard_map/all_gather | solution.py:111
  117.2 1.0 copy.32
  118.8 11.7 %cholesky.104 = f32[128,128]{1,0:T(8,128)S(1)} custom-call(f32[128,128]{1,0:T(8,128)S(1)} %cholesky.266), custom_call_target="Cholesky" | custom-call | tf_op jit(solution)/shard_map/jit(cholesky)/cholesky | solution.py:121
  130.5 9.8 %custom-call.34 = f32[1,128,128]{1,2,0:T(8,128)S(1)} custom-call(f32[1,128,128]{2,1,0:T(8,128)S(1)} %get-tuple-element.32), custom_call_target="InvertDiagBlocksLowerTriangular" | custom-call | tf_op jit(solution)/shard_map/jit(cholesky)/cholesky | solution.py:121
  141.2 11.7 %cholesky.217 = f32[128,128]{1,0:T(8,128)S(1)} custom-call(f32[128,128]{1,0:T(8,128)S(1)} %cholesky.270), custom_call_target="Cholesky" | custom-call | tf_op jit(solution)/shard_map/jit(cholesky)/cholesky | solution.py:121
  152.9 9.9 %custom-call.35 = f32[1,128,128]{1,2,0:T(8,128)S(1)} custom-call(f32[1,128,128]{2,1,0:T(8,128)S(1)} %get-tuple-element.29), custom_call_target="InvertDiagBlocksLowerTriangular" | custom-call | tf_op jit(solution)/shard_map/jit(cholesky)/cholesky | solution.py:121
  163.9 12.2 %all-gather = bf16[32,2048]{1,0:T(8,128)(2,1)} all-gather(bf16[8,2048]{1,0:T(8,128)(2,1)S(1)} %gather_fusion.3), channel_id=2, replica_groups=mesh['tri_0'=4,'tri_1'=16,'sub'=8] {'tri_0'}, dimensions={0}, use_global_device_ids=true | all-gather | bytes 163840 | tf_op jit(solution)/shard_map/all_gather | solution.py:22
  176.1 1.2 convolution_dynamic-update-slice_fusion
  177.7 11.7 %cholesky.238 = f32[128,128]{1,0:T(8,128)S(1)} custom-call(f32[128,128]{1,0:T(8,128)S(1)} %cholesky.275), custom_call_target="Cholesky" | custom-call | tf_op jit(solution)/shard_map/jit(cholesky)/cholesky | solution.py:121
  189.4 9.8 %custom-call.36 = f32[1,128,128]{1,2,0:T(8,128)S(1)} custom-call(f32[1,128,128]{2,1,0:T(8,128)S(1)} %get-tuple-element.26), custom_call_target="InvertDiagBlocksLowerTriangular" | custom-call | tf_op jit(solution)/shard_map/jit(cholesky)/cholesky | solution.py:121
  199.8 11.7 %cholesky.255 = f32[128,128]{1,0:T(8,128)S(1)} custom-call(f32[128,128]{1,0:T(8,128)S(1)} %convolution_subtract_fusion.8), custom_call_target="Cholesky" | custom-call | tf_op jit(solution)/shard_map/jit(cholesky)/cholesky | solution.py:121
  216.6 10.2 %while.1 = (s32[]{:T(128)}, f32[512,512]{1,0:T(8,128)S(1)}, s32[4,2]{0,1:T(2,128)S(1)}, f32[4,128,128]{2,1,0:T(8,128)}, s32[]{:T(128)}) while((s32[]{:T(128)}, f32[512,512]{1,0:T(8,128)S(1)}, s32[4,2]{0,1:T(2,128)S(1)}, f32[4,128,128]{2,1,0:T(8,128)}, s32[]{:T(128)}) %tuple.28), condition=%wide.while_cond, body=%wide.while_body.sunk | while | flops 2 | bytes 132705 | solution.py:122
  217.4 1.9 bitcast_dynamic-update-slice_fusion.2
  219.9 1.9 bitcast_dynamic-update-slice_fusion.2
  222.4 1.9 bitcast_dynamic-update-slice_fusion.2
  224.9 1.9 bitcast_dynamic-update-slice_fusion.2
  226.8 40.1 %custom-call.37 = f32[4,128,128]{1,2,0:T(8,128)S(1)} custom-call(f32[4,128,128]{2,1,0:T(8,128)} %get-tuple-element.12), custom_call_target="InvertDiagBlocksLowerTriangular" | custom-call | tf_op jit(solution)/shard_map/jit(_cho_solve)/triangular_solve | solution.py:122
  267.3 1.1 bitcast_convert_fusion
  268.4 1.7 copy.27
  270.1 1.2 copy.28
  271.3 2.6 reshape_reshape.6
  273.9 1.0 dynamic-slice_bitcast_fusion
  274.9 1.3 convolution_subtract_fusion.3
  276.2 1.3 fusion.49
  277.5 4.4 %collective-permute-done = bf16[4,64,512]{2,1,0:T(8,128)(2,1)S(1)} collective-permute-done((bf16[4,64,512]{2,1,0:T(8,128)(2,1)S(1)}, bf16[4,64,512]{2,1,0:T(8,128)(2,1)S(1)}, u32[]{:S(2)}, u32[]{:S(2)}) %collective-permute-start) | collective-permute-done | bytes 262176 | tf_op jit(solution)/shard_map/ppermute | solution.py:116
  281.9 1.4 convolution_subtract_fusion.2
  283.3 1.3 fusion.51
  284.5 4.4 %collective-permute-done.1 = bf16[4,64,512]{2,1,0:T(8,128)(2,1)S(1)} collective-permute-done((bf16[4,64,512]{2,1,0:T(8,128)(2,1)S(1)}, bf16[4,64,512]{2,1,0:T(8,128)(2,1)S(1)}, u32[]{:S(2)}, u32[]{:S(2)}) %collective-permute-start.1) | collective-permute-done | bytes 262176 | tf_op jit(solution)/shard_map/ppermute | solution.py:116
  288.9 1.6 convolution_subtract_fusion.5
  290.9 5.0 %collective-permute-done.2 = bf16[4,64,512]{2,1,0:T(8,128)(2,1)S(1)} collective-permute-done((bf16[4,64,512]{2,1,0:T(8,128)(2,1)S(1)}, bf16[4,64,512]{2,1,0:T(8,128)(2,1)S(1)}, u32[]{:S(2)}, u32[]{:S(2)}) %collective-permute-start.2) | collective-permute-done | bytes 262176 | tf_op jit(solution)/shard_map/ppermute | solution.py:116
  296.7 6.2 %collective-permute-done.3 = bf16[4,64,512]{2,1,0:T(8,128)(2,1)S(1)} collective-permute-done((bf16[4,64,512]{2,1,0:T(8,128)(2,1)S(1)}, bf16[4,64,512]{2,1,0:T(8,128)(2,1)S(1)}, u32[]{:S(2)}, u32[]{:S(2)}) %collective-permute-start.3) | collective-permute-done | bytes 262176 | tf_op jit(solution)/shard_map/ppermute | solution.py:116
  303.8 6.2 %collective-permute-done.4 = bf16[4,64,512]{2,1,0:T(8,128)(2,1)S(1)} collective-permute-done((bf16[4,64,512]{2,1,0:T(8,128)(2,1)S(1)}, bf16[4,64,512]{2,1,0:T(8,128)(2,1)S(1)}, u32[]{:S(2)}, u32[]{:S(2)}) %collective-permute-start.4) | collective-permute-done | bytes 262176 | tf_op jit(solution)/shard_map/ppermute | solution.py:116
  311.0 6.0 %collective-permute-done.5 = bf16[4,64,512]{2,1,0:T(8,128)(2,1)S(1)} collective-permute-done((bf16[4,64,512]{2,1,0:T(8,128)(2,1)S(1)}, bf16[4,64,512]{2,1,0:T(8,128)(2,1)S(1)}, u32[]{:S(2)}, u32[]{:S(2)}) %collective-permute-start.5) | collective-permute-done | bytes 262176 | tf_op jit(solution)/shard_map/ppermute | solution.py:116
  317.3 1.6 convolution_convert_fusion
  318.9 1.5 gather_fusion.4
  320.4 3.5 %collective-permute-done.6 = bf16[4,64,512]{2,1,0:T(8,128)(2,1)S(1)} collective-permute-done((bf16[4,64,512]{2,1,0:T(8,128)(2,1)S(1)}, bf16[4,64,512]{2,1,0:T(8,128)(2,1)S(1)}, u32[]{:S(2)}, u32[]{:S(2)}) %collective-permute-start.6) | collective-permute-done | bytes 262176 | tf_op jit(solution)/shard_map/ppermute | solution.py:116
  324.1 1.0 constant_dynamic-update-slice_fusion.8
  326.4 3.7 %gather_fusion.5 = bf16[10,512,512]{2,1,0:T(8,128)(2,1)} fusion(bf16[4,512,512]{2,1,0:T(8,128)(2,1)S(1)} %constant_dynamic-slice_fusion.1, s32[1024]{0:T(1024)S(1)} %get-tuple-element.35), kind=kCustom, calls=%fused_computation.5 | custom fusion | bytes 10485800 | tf_op jit(solution)/shard_map/gather | solution.py:127
  330.2 5.4 %fusion.1 = f32[1,10,64,512]{3,2,1,0:T(8,128)} fusion(bf16[10,64,512]{2,1,0:T(8,128)(2,1)} %gather_fusion.4, bf16[10,512,512]{2,1,0:T(8,128)(2,1)} %gather_fusion.5, pred[10]{0:T(512)(128)(4,1)S(1)} %and_bitcast_fusion, f32[1,10,64,512]{3,2,1,0:T(8,128)S(1)} %copy-done), kind=kOutput, calls=%fused_computation.10 | convolution fusion | flops 336199680 | bytes 8519690 | tf_op jit(solution)/shard_map/qrk,qck->qrc/dot_general | solution.py:128
  (104 shorter events, 22.0 us)
Async XLA Ops:
  11.3 35.0 %all-to-all-start.1 = ((bf16[64,2,256]{2,1,0:T(2,128)(2,1)}), bf16[64,2,256]{2,1,0:T(2,128)(2,1)S(1)}, u32[]{:S(2)}, u32[]{:S(2)}) async-start(bf16[64,2,256]{2,1,0:T(2,128)(2,1)} %reshape.304), calls=%async_computation.1 | async-start | bytes 131072 | tf_op jit(solution)/shard_map/all_to_all | solution.py:99
  46.3 116.6 %all-to-all-start = ((bf16[64,2,1024]{2,1,0:T(2,128)(2,1)}), bf16[64,2,1024]{2,1,0:T(2,128)(2,1)S(1)}, u32[]{:S(2)}, u32[]{:S(2)}) async-start(bf16[64,2,1024]{2,1,0:T(2,128)(2,1)} %reshape.306), calls=%async_computation | async-start | bytes 524288 | tf_op jit(solution)/shard_map/all_to_all | solution.py:96
  61.4 206.9 %all-gather.3.cloned.1.call-start = ((), (), s32[]{:S(2)}) async-start(), calls=%async_computation.2 | async-start | bytes 2228224 | tf_op jit(solution)/shard_map/all_gather | solution.py:22
  140.8 126.1 %copy-start.1 = (bf16[512,512]{0,1:T(8,128)(2,1)S(1)}, bf16[512,512]{0,1:T(8,128)(2,1)}, u32[]{:S(2)}) copy-start(bf16[512,512]{0,1:T(8,128)(2,1)} %copy.32) | copy-start | bytes 1572868
  141.1 21.7 %copy-start.4 = (f32[384,128]{1,0:T(8,128)}, f32[384,128]{1,0:T(8,128)S(1)}, u32[]{:S(2)}) copy-start(f32[384,128]{1,0:T(8,128)S(1)} %convolution_subtract_fusion.6) | copy-start | bytes 589828
  266.9 3.2 copy-start.2
  273.9 16.6 %copy-start.3 = (f32[4,128,128]{1,2,0:T(8,128)S(1)}, f32[4,128,128]{1,2,0:T(8,128)}, u32[]{:S(2)}) copy-start(f32[4,128,128]{1,2,0:T(8,128)} %copy-done.2) | copy-start | bytes 786436
  274.9 7.0 %collective-permute-start = (bf16[4,64,512]{2,1,0:T(8,128)(2,1)S(1)}, bf16[4,64,512]{2,1,0:T(8,128)(2,1)S(1)}, u32[]{:S(2)}, u32[]{:S(2)}) collective-permute-start(bf16[4,64,512]{2,1,0:T(8,128)(2,1)S(1)} %dynamic-slice_bitcast_fusion), channel_id=1, source_target_pairs={{0,1},{1,2},{2,3},{3,4},{4,5},{5,6},{6,7},{7,0},{8,9},{9,10},{10,1... | collective-permute-start | bytes 786440 | tf_op jit(solution)/shard_map/ppermute | solution.py:116
  281.9 7.0 %collective-permute-start.1 = (bf16[4,64,512]{2,1,0:T(8,128)(2,1)S(1)}, bf16[4,64,512]{2,1,0:T(8,128)(2,1)S(1)}, u32[]{:S(2)}, u32[]{:S(2)}) collective-permute-start(bf16[4,64,512]{2,1,0:T(8,128)(2,1)S(1)} %collective-permute-done), channel_id=1, source_target_pairs={{0,1},{1,2},{2,3},{3,4},{4,5},{5,6},{6,7},{7,0},{8,9},{9,10},{10,1... | collective-permute-start | bytes 786440 | tf_op jit(solution)/shard_map/ppermute | solution.py:116
  288.9 7.0 %collective-permute-start.2 = (bf16[4,64,512]{2,1,0:T(8,128)(2,1)S(1)}, bf16[4,64,512]{2,1,0:T(8,128)(2,1)S(1)}, u32[]{:S(2)}, u32[]{:S(2)}) collective-permute-start(bf16[4,64,512]{2,1,0:T(8,128)(2,1)S(1)} %collective-permute-done.1), channel_id=1, source_target_pairs={{0,1},{1,2},{2,3},{3,4},{4,5},{5,6},{6,7},{7,0},{8,9},{9,10},{10,1... | collective-permute-start | bytes 786440 | tf_op jit(solution)/shard_map/ppermute | solution.py:116
  295.9 7.0 %collective-permute-start.3 = (bf16[4,64,512]{2,1,0:T(8,128)(2,1)S(1)}, bf16[4,64,512]{2,1,0:T(8,128)(2,1)S(1)}, u32[]{:S(2)}, u32[]{:S(2)}) collective-permute-start(bf16[4,64,512]{2,1,0:T(8,128)(2,1)S(1)} %collective-permute-done.2), channel_id=1, source_target_pairs={{0,1},{1,2},{2,3},{3,4},{4,5},{5,6},{6,7},{7,0},{8,9},{9,10},{10,1... | collective-permute-start | bytes 786440 | tf_op jit(solution)/shard_map/ppermute | solution.py:116
  302.9 7.0 %collective-permute-start.4 = (bf16[4,64,512]{2,1,0:T(8,128)(2,1)S(1)}, bf16[4,64,512]{2,1,0:T(8,128)(2,1)S(1)}, u32[]{:S(2)}, u32[]{:S(2)}) collective-permute-start(bf16[4,64,512]{2,1,0:T(8,128)(2,1)S(1)} %collective-permute-done.3), channel_id=1, source_target_pairs={{0,1},{1,2},{2,3},{3,4},{4,5},{5,6},{6,7},{7,0},{8,9},{9,10},{10,1... | collective-permute-start | bytes 786440 | tf_op jit(solution)/shard_map/ppermute | solution.py:116
  309.9 7.0 %collective-permute-start.5 = (bf16[4,64,512]{2,1,0:T(8,128)(2,1)S(1)}, bf16[4,64,512]{2,1,0:T(8,128)(2,1)S(1)}, u32[]{:S(2)}, u32[]{:S(2)}) collective-permute-start(bf16[4,64,512]{2,1,0:T(8,128)(2,1)S(1)} %collective-permute-done.4), channel_id=1, source_target_pairs={{0,1},{1,2},{2,3},{3,4},{4,5},{5,6},{6,7},{7,0},{8,9},{9,10},{10,1... | collective-permute-start | bytes 786440 | tf_op jit(solution)/shard_map/ppermute | solution.py:116
  316.9 7.0 %collective-permute-start.6 = (bf16[4,64,512]{2,1,0:T(8,128)(2,1)S(1)}, bf16[4,64,512]{2,1,0:T(8,128)(2,1)S(1)}, u32[]{:S(2)}, u32[]{:S(2)}) collective-permute-start(bf16[4,64,512]{2,1,0:T(8,128)(2,1)S(1)} %collective-permute-done.5), channel_id=1, source_target_pairs={{0,1},{1,2},{2,3},{3,4},{4,5},{5,6},{6,7},{7,0},{8,9},{9,10},{10,1... | collective-permute-start | bytes 786440 | tf_op jit(solution)/shard_map/ppermute | solution.py:116
  326.4 3.8 %copy-start = (f32[1,10,64,512]{3,2,1,0:T(8,128)S(1)}, f32[1,10,64,512]{3,2,1,0:T(8,128)}, u32[]{:S(2)}) copy-start(f32[1,10,64,512]{3,2,1,0:T(8,128)} %param.9) | copy-start | bytes 3932164
Sparse Core Ops, SparseCore 0:
  176.2 70.5 all-gather.2
